TPU v7x, 32 devices: a whole 2x2x4 slice. The times are simulated.
32 devices in a mesh: ctx: 16 (over z, y, core), tp: 2 (over x).
Axes of the slice: x: 2, y: 2, z: 4, core: 2. Of those that a mesh axis runs over, the one named last changes fastest.
Arguments:
- queries: bfloat16 [64, 2, 8192], P('ctx', None, 'tp'), may hold values from -60 to 60
- new_keys: bfloat16 [2, 64, 1024], P(None, 'ctx', 'tp'), may hold values from -9.5625 to 9.5625
- new_values: bfloat16 [2, 64, 1024], P(None, 'ctx', 'tp'), may hold values from -6 to 6
- cache_keys: bfloat16 [2, 65536, 1024], P(None, 'ctx', 'tp'), may hold values from -6 to 6
- cache_values: bfloat16 [2, 65536, 1024], P(None, 'ctx', 'tp'), may hold values from -6 to 6
- hist_len: int32 [2], replicated, may hold values from 16384 to 61440, as said below
- page_owner: int32 [2, 16], replicated, may hold values from 0 to 15, as said below
- out_weight: bfloat16 [8192, 8192], P('tp', 'ctx'), may hold values from -0.0625 to 0.0625
Outputs:
- attended: bfloat16 [64, 2, 8192], P('tp', None, 'ctx')
- stored_keys: bfloat16 [16, 2, 4, 1024], P('ctx', None, None, 'tp')
- stored_values: bfloat16 [16, 2, 4, 1024], P('ctx', None, None, 'tp')
Inputs may be any that keep to these rules, and one draw needn't show every extreme that they name: `hist_len`: some request has the full length. `page_owner`: each row lists every device once; page b of request r holds its new-turn tokens b * 4 to (b + 1) * 4 - 1; some column b holds one value in every row.
All inputs are finite; a program needn't handle non-finite values.
Results may differ from a plain program's by a relative error of at most 0.0085.
Values may be sent and summed in bfloat16 or wider, within the bound.
No kernel may reach another device: no remote copies, remote signals or barrier semaphores. Data moves between devices by JAX's collectives and lax.ppermute only.
A program may use at most 64 MiB of HBM per device.

v0:
```python
import math

import jax
import jax.numpy as jnp
from jax import lax
from jax.sharding import PartitionSpec as P

HD = 128


FLOOR_SCORE = -1e30


def online_step(progress, scores, value_block, visible):
    accumulated, peak_score, running_total = progress
    masked = jnp.where(visible, scores, FLOOR_SCORE)
    new_peak = jnp.maximum(peak_score, jnp.max(masked, axis=-1))
    shrink = jnp.exp(peak_score - new_peak)
    weights = jnp.where(visible, jnp.exp(masked - new_peak[..., None]), 0.0)
    running_total = running_total * shrink + jnp.sum(weights, axis=-1)
    update = jnp.einsum(
        "nrkgb,rbkd->nrkgd",
        weights.astype(jnp.bfloat16),
        value_block,
        preferred_element_type=jnp.float32,
    )
    accumulated = accumulated * shrink[..., None] + update
    return (accumulated, new_peak, running_total)


def on_device(
    queries, new_keys, new_values, cache_keys, cache_values, hist_len, page_owner, out_weight
):
    members = lax.axis_size("ctx")
    own_index = lax.axis_index("ctx")
    requests, page_rows, kv_width = new_keys.shape
    heads_width = queries.shape[2]
    head_size = HD
    kv_heads = kv_width // head_size
    group_size = heads_width // kv_width
    history = cache_keys.shape[1]
    half_size = history // 2
    turn_total = page_rows * members
    key_block = min(512, half_size)
    block_count = history // key_block
    score_scale = 1.0 / math.sqrt(head_size)
    owner_row = lax.dynamic_index_in_dim(page_owner, own_index, 1, keepdims=False)
    device_ids = jnp.arange(members, dtype=jnp.int32)
    targets = (owner_row[None, :] == device_ids[:, None]).astype(jnp.bfloat16)
    send_keys = targets[:, :, None, None] * new_keys[None]
    send_values = targets[:, :, None, None] * new_values[None]
    got_keys, got_values = (
        lax.all_to_all(send_keys, "ctx", split_axis=0, concat_axis=0, tiled=True),
        lax.all_to_all(send_values, "ctx", split_axis=0, concat_axis=0, tiled=True),
    )
    own_keys = jnp.sum(got_keys, axis=0)
    own_values = jnp.sum(got_values, axis=0)
    mine_mask = (page_owner == own_index).astype(jnp.int32)
    anchor = jnp.sum(mine_mask * device_ids[None, :], axis=1)
    key_turn = anchor[:, None] * page_rows + jnp.arange(page_rows, dtype=jnp.int32)[None, :]
    own_keys4 = own_keys.reshape(requests, page_rows, kv_heads, head_size)
    own_values4 = own_values.reshape(requests, page_rows, kv_heads, head_size)
    local_slot = jnp.arange(history, dtype=jnp.int32)
    position = jnp.where(
        local_slot < half_size,
        own_index * half_size + local_slot,
        (2 * members - 1 - own_index) * half_size + local_slot - half_size,
    )
    alive_slot = position[None, :] < hist_len[:, None]
    query_piece = lax.all_gather(queries, "ctx", axis=0, tiled=True)
    row_count = query_piece.shape[0]
    grouped = query_piece.reshape(row_count, requests, kv_heads, group_size, head_size)
    start_state = (
        jnp.zeros((row_count, requests, kv_heads, group_size, head_size), jnp.float32),
        jnp.full((row_count, requests, kv_heads, group_size), FLOOR_SCORE, jnp.float32),
        jnp.zeros((row_count, requests, kv_heads, group_size), jnp.float32),
    )

    def visit(step_index, progress):
        offset = step_index * key_block
        key_slab = lax.dynamic_slice_in_dim(cache_keys, offset, key_block, 1).reshape(
            requests, key_block, kv_heads, head_size
        )
        value_slab = lax.dynamic_slice_in_dim(cache_values, offset, key_block, 1).reshape(
            requests, key_block, kv_heads, head_size
        )
        live_slab = lax.dynamic_slice_in_dim(alive_slot, offset, key_block, 1)
        scores = (
            jnp.einsum("nrkgd,rbkd->nrkgb", grouped, key_slab, preferred_element_type=jnp.float32)
            * score_scale
        )
        return online_step(progress, scores, value_slab, live_slab[None, :, None, None, :])

    progress = lax.fori_loop(0, block_count, visit, start_state)
    query_turn = jnp.arange(row_count, dtype=jnp.int32)
    scores = (
        jnp.einsum("nrkgd,rbkd->nrkgb", grouped, own_keys4, preferred_element_type=jnp.float32)
        * score_scale
    )
    visible = (key_turn[None, :, :] <= query_turn[:, None, None])[:, :, None, None, :]
    progress = online_step(progress, scores, own_values4, visible)
    accumulated, peak_score, running_total = tuple((piece for piece in progress))
    global_peak = lax.pmax(peak_score, "ctx")
    weight = jnp.exp(peak_score - global_peak)
    global_total = lax.psum(running_total * weight, "ctx")
    shared_rows = lax.psum_scatter(
        accumulated * (weight / global_total)[..., None], "ctx", scatter_dimension=0, tiled=True
    )
    attention = lax.all_gather(shared_rows.astype(jnp.bfloat16), "ctx", axis=0, tiled=True)
    flattened = attention.reshape(turn_total, requests, heads_width)
    attended = lax.psum_scatter(
        jnp.einsum("trc,cd->trd", flattened, out_weight, preferred_element_type=jnp.float32),
        "tp",
        scatter_dimension=0,
        tiled=True,
    ).astype(jnp.bfloat16)
    return (attended, own_keys[None], own_values[None])


def solution(mesh):
    return jax.shard_map(
        on_device,
        mesh=mesh,
        in_specs=(
            P("ctx", None, "tp"),
            P(None, "ctx", "tp"),
            P(None, "ctx", "tp"),
            P(None, "ctx", "tp"),
            P(None, "ctx", "tp"),
            P(),
            P(),
            P("tp", "ctx"),
        ),
        out_specs=(P("tp", None, "ctx"), P("ctx", None, None, "tp"), P("ctx", None, None, "tp")),
        check_vma=False,
    )
```

profile of v0, /device:TPU:0, one launch (start us, length us, event | category | flops | bytes accessed | tf_op | source)
XLA Modules:
  0.0 395.3 jit_solution(15229869160162841402)
XLA Ops:
  10.4 7.4 %all-to-all-start.1 = ((bf16[16,2,4,512]{3,2,1,0:T(4,128)(2,1)}), bf16[16,2,4,512]{3,2,1,0:T(4,128)(2,1)S(1)}, u32[]{:S(2)}, u32[]{:S(2)}) async-start(bf16[16,2,4,512]{3,2,1,0:T(4,128)(2,1)} %get-tuple-element.245), calls=%async_computation.1 | async-start | bytes 262144 | tf_op jit(solution)/shard_map/all_to_all | solution.py:54
  19.3 6.4 %all-to-all-done.1 = bf16[16,2,4,512]{3,2,1,0:T(4,128)(2,1)S(1)} async-done(((bf16[16,2,4,512]{3,2,1,0:T(4,128)(2,1)}), bf16[16,2,4,512]{3,2,1,0:T(4,128)(2,1)S(1)}, u32[]{:S(2)}, u32[]{:S(2)}) %all-to-all-start.1) | async-done | bytes 131104 | tf_op jit(solution)/shard_map/all_to_all | solution.py:54
  25.7 3.5 all-to-all-start
  29.5 7.6 %all-to-all-done = bf16[16,2,4,512]{3,2,1,0:T(4,128)(2,1)S(1)} async-done(((bf16[16,2,4,512]{3,2,1,0:T(4,128)(2,1)}), bf16[16,2,4,512]{3,2,1,0:T(4,128)(2,1)S(1)}, u32[]{:S(2)}, u32[]{:S(2)}) %all-to-all-start) | async-done | bytes 131104 | tf_op jit(solution)/shard_map/all_to_all | solution.py:53
  37.2 13.7 %all-gather.3.cloned.1.call-done = bf16[64,2,4096]{2,1,0:T(2,128)(2,1)} async-done(((bf16[4,2,4096]{2,1,0:T(2,128)(2,1)}), bf16[64,2,4096]{2,1,0:T(2,128)(2,1)}) %all-gather.3.cloned.1.call-update) | async-done | bytes 1048592 | tf_op jit(solution)/shard_map/all_gather | solution.py:70
  53.7 93.4 %while.18 = (s32[]{:T(128)}, f32[64,2,4,8,128]{4,0,3,2,1:T(8,128)}, f32[64,2,4,8]{0,3,2,1:T(8,128)S(1)}, f32[64,2,4,8]{0,3,2,1:T(8,128)S(1)}, pred[2,4096]{1,0:T...) while((s32[]{:T(128)}, f32[64,2,4,8,128]{4,0,3,2,1:T(8,128)}, ...), condition=%wide.region_3.4_spmd.clone, body=%wide.region_0.3_spmd.clone.sunk | while | flops 1102598144 | bytes 62133520 | solution.py:94
  61.1 2.9 bitcast_add_fusion.3
  70.3 2.4 fusion.47
  72.8 2.9 bitcast_add_fusion.3
  84.4 2.9 bitcast_add_fusion.3
  93.7 2.4 fusion.47
  96.1 2.9 bitcast_add_fusion.3
  107.8 2.9 bitcast_add_fusion.3
  119.5 2.9 bitcast_add_fusion.3
  131.2 2.9 bitcast_add_fusion.3
  142.8 2.9 bitcast_add_fusion.3
  149.3 59.6 %pmax.7 = f32[64,2,4,8]{0,3,2,1:T(8,128)S(1)} all-reduce(f32[64,2,4,8]{0,3,2,1:T(8,128)S(1)} %max.12), channel_id=1, replica_groups=mesh['ctx'=16,'tp'=2] {'ctx'}, use_global_device_ids=true, to_apply=%region_8.9 | all-reduce | flops 4096 | bytes 32768 | tf_op jit(solution)/shard_map/pmax | solution.py:103
  209.1 57.6 %psum.7 = f32[64,2,4,8]{0,3,2,1:T(8,128)S(1)} all-reduce(f32[64,2,4,8]{0,3,2,1:T(8,128)S(1)} %get-tuple-element.239), channel_id=1, replica_groups=mesh['ctx'=16,'tp'=2] {'ctx'}, use_global_device_ids=true, to_apply=%region_10.11 | all-reduce | flops 4096 | bytes 32768 | tf_op jit(solution)/shard_map/psum | solution.py:105
  266.8 2.8 fusion.16
  269.6 2.6 copy.60
  272.2 58.9 %reduce-scatter.3.cloned.1.call-done = f32[4,2,4,8,128]{4,3,2,1,0:T(8,128)} async-done(((f32[64,2,4,8,128]{4,3,2,1,0:T(8,128)}), f32[4,2,4,8,128]{4,3,2,1,0:T(8,128)}) %reduce-scatter.3.cloned.1.call-update) | async-done | bytes 131088 | tf_op jit(solution)/shard_map/reduce_scatter | solution.py:106
  332.8 38.3 %all-gather.5.cloned.1.call-done = bf16[64,2,4,8,128]{4,3,2,1,0:T(8,128)(2,1)} async-done(((bf16[4,2,4,8,128]{4,3,2,1,0:T(8,128)(2,1)}), bf16[64,2,4,8,128]{4,3,2,1,0:T(8,128)(2,1)}) %all-gather.5.cloned.1.call-update) | async-done | bytes 1048592 | tf_op jit(solution)/shard_map/all_gather | solution.py:109
  372.5 3.9 fusion.14
  376.4 10.7 %reduce-scatter.5.cloned.1.call-done = f32[32,2,512]{2,0,1:T(8,128)} async-done(((f32[64,2,512]{2,0,1:T(8,128)}), f32[32,2,512]{2,0,1:T(8,128)}) %reduce-scatter.5.cloned.1.call-update) | async-done | bytes 131088 | tf_op jit(solution)/shard_map/reduce_scatter | solution.py:111
  (157 shorter events, 79.5 us)
Async XLA Ops:
  7.2 43.7 %all-gather.3.cloned.1.call-start = ((), (), s32[]{:S(2)}) async-start(), calls=%async_computation.4 | async-start | bytes 1114112 | tf_op jit(solution)/shard_map/all_gather | solution.py:70
  10.4 15.3 %all-to-all-start.1 = ((bf16[16,2,4,512]{3,2,1,0:T(4,128)(2,1)}), bf16[16,2,4,512]{3,2,1,0:T(4,128)(2,1)S(1)}, u32[]{:S(2)}, u32[]{:S(2)}) async-start(bf16[16,2,4,512]{3,2,1,0:T(4,128)(2,1)} %get-tuple-element.245), calls=%async_computation.1 | async-start | bytes 262144 | tf_op jit(solution)/shard_map/all_to_all | solution.py:54
  25.7 11.4 %all-to-all-start = ((bf16[16,2,4,512]{3,2,1,0:T(4,128)(2,1)}), bf16[16,2,4,512]{3,2,1,0:T(4,128)(2,1)S(1)}, u32[]{:S(2)}, u32[]{:S(2)}) async-start(bf16[16,2,4,512]{3,2,1,0:T(4,128)(2,1)} %get-tuple-element.246), calls=%async_computation | async-start | bytes 262144 | tf_op jit(solution)/shard_map/all_to_all | solution.py:53
  29.2 302.0 %reduce-scatter.3.cloned.1.call-start = ((), (), s32[]{:S(2)}) async-start(), calls=%async_computation.5 | async-start | bytes 2228224 | tf_op jit(solution)/shard_map/reduce_scatter | solution.py:106
  29.5 237.3 %copy-start.4 = (bf16[2,4,512]{2,1,0:T(4,128)(2,1)}, bf16[2,4,512]{2,1,0:T(4,128)(2,1)S(1)}, u32[]{:S(2)}) copy-start(bf16[2,4,512]{2,1,0:T(4,128)(2,1)S(1)} %reduce_sum.57) | copy-start | bytes 24580
  37.2 110.0 %copy-start.5 = (bf16[2,4,512]{2,1,0:T(4,128)(2,1)}, bf16[2,4,512]{2,1,0:T(4,128)(2,1)S(1)}, u32[]{:S(2)}) copy-start(bf16[2,4,512]{2,1,0:T(4,128)(2,1)S(1)} %reduce_sum.56) | copy-start | bytes 24580
  58.6 2.4 copy-start
  58.6 2.4 copy-start.2
  70.3 2.4 copy-start
  70.3 2.4 copy-start.2
  82.0 2.4 copy-start
  82.0 2.4 copy-start.2
  93.7 2.4 copy-start
  93.7 2.4 copy-start.2
  105.3 2.4 copy-start
  105.4 2.4 copy-start.2
  117.0 2.4 copy-start
  117.0 2.4 copy-start.2
  128.7 2.4 copy-start
  128.7 2.4 copy-start.2
  140.4 2.4 copy-start
  140.4 2.4 copy-start.2
  272.2 98.9 %all-gather.5.cloned.1.call-start = ((), (), s32[]{:S(2)}) async-start(), calls=%async_computation.6 | async-start | bytes 1114112 | tf_op jit(solution)/shard_map/all_gather | solution.py:109
  332.7 54.4 %reduce-scatter.5.cloned.1.call-start = ((), (), s32[]{:S(2)}) async-start(), calls=%async_computation.7 | async-start | bytes 393216 | tf_op jit(solution)/shard_map/reduce_scatter | solution.py:111
  (9 other events, 11.8 us)
Sparse Core Ops, SparseCore 0:
  10.2 40.6 all-gather.2
  272.3 58.8 reduce-scatter.2
  334.1 36.9 all-gather.4
  376.5 10.5 reduce-scatter.4
where the time goes:
time: 396 us; the launch traced here: 395 us
  waiting for transfers between devices  136 us (34%)
  blocking collectives  117 us (30%)
  local copies, waits for them, and re-layouts  47.5 us (12%)
  matrix products  43.1 us (11%)
  other arithmetic  25.3 us (6%)
  between operations  13.9 us (4%)
  starting transfers between devices  11.1 us (3%)
    pmax x1, blocking collectives, on_device(): global_peak = lax.pmax(peak_score, 'ctx')  59.6 us
    reduce_scatter x1, waiting for transfers between devices, on_device(): lax.psum_scatter(accumulated * (weight / global_total)[..., None], 'ctx',...  58.9 us
    psum x1, blocking collectives, on_device(): global_total = lax.psum(running_total * weight, 'ctx')  57.6 us
    all_gather x1, waiting for transfers between devices, on_device(): lax.all_gather(shared_rows.astype(jnp.bfloat16), 'ctx', axis=0, tiled=True)  38.3 us
    dot_general x9, matrix products, online_step(): jnp.einsum('nrkgb,rbkd->nrkgd', weights.astype(jnp.bfloat16), value_block...  26.2 us
    dynamic_slice x16, local copies, waits for them, and re-layouts, visit(): lax.dynamic_slice_in_dim(cache_values, offset, key_block, 1)  24.2 us
    reduce_sum x9, other arithmetic, online_step(): running_total = running_total * shrink + jnp.sum(weights, axis=-1)  19.2 us
    all_gather x1, waiting for transfers between devices, on_device(): query_piece = lax.all_gather(queries, 'ctx', axis=0, tiled=True)  13.7 us
  transfers between devices with their start and end apart: 6, of which 6 were waited for; matrix products, arithmetic and copies ran while one was open for 1% of the time, Pallas kernels for 0%

commit v1 on v0

--- a/solution.py
+++ b/solution.py
@@ -1,8 +1,11 @@
+import functools
 import math
 
 import jax
 import jax.numpy as jnp
 from jax import lax
+from jax.experimental import pallas as pl
+from jax.experimental.pallas import tpu as pltpu
 from jax.sharding import PartitionSpec as P
 
 HD = 128
@@ -117,20 +120,382 @@
     return (attended, own_keys[None], own_values[None])
 
 
+F32 = jnp.float32
+BF16 = jnp.bfloat16
+NT = (((1,), (1,)), ((), ()))
+TN = (((0,), (0,)), ((), ()))
+LOG2_SCALE = math.log2(math.e) / math.sqrt(HD)
+FLOOR_EXP = -float(2**20)
+SUM_LIMIT = float(2**100)
+STAT_ROWS = 16
+VMEM_LIMIT = 56 << 20
+
+
+def pack_stats(ref_exp, total):
+    high = jnp.floor(ref_exp * (1 / 64)) * 64
+    total_high = total.astype(BF16).astype(F32)
+    row = lax.broadcasted_iota(jnp.int32, (STAT_ROWS, ref_exp.shape[1]), 0)
+    rest = jnp.where(row == 2, total_high, jnp.where(row == 3, total - total_high, 0.0))
+    return jnp.where(row == 0, high, jnp.where(row == 1, ref_exp - high, rest)).astype(BF16)
+
+
+def unpack(part):
+    stats = part[HD:, :].astype(F32)
+    return part[:HD, :].astype(F32), stats[0:1, :] + stats[1:2, :], stats[2:3, :] + stats[3:4, :]
+
+
+def combine(parts):
+    parts = [unpack(part) for part in parts]
+    top = functools.reduce(jnp.maximum, [part[1] for part in parts])
+    shrinks = [jnp.exp2(part[1] - top) for part in parts]
+    summed = sum(part[0] * shrink for part, shrink in zip(parts, shrinks))
+    total = sum(part[2] * shrink for part, shrink in zip(parts, shrinks))
+    return summed, top, total
+
+
+def attend_kernel(
+    grid_z, group, info, line_own, line_other, far_own, far_other, turn_keys, turn_values,
+    key_block, value_block, all_keys, all_values, out, q, acc, exps, sums, key_slab, value_slab, sems,
+):
+    step_r, j = pl.program_id(0), pl.program_id(1)
+    requests, kv_heads, lanes, _ = q.shape
+    own, z, y, c = info[4], info[5], info[6], info[7]
+    r = lax.rem(step_r + c + 1, 2)
+    block = key_block.shape[1]
+    history = all_keys.shape[1]
+    half = history // 2
+    page = turn_keys.shape[1]
+    piece = line_own.shape[3]
+    n_first, n_second = info[2 * r], info[2 * r + 1]
+
+    @pl.when((step_r == 0) & (j == 0))
+    def _():
+        copies = []
+        for k in range(grid_z):
+            source_z = lax.rem(z - k + grid_z, grid_z)
+            for at_y, at_c, ref in (
+                (y, c, line_own), (y, 1 - c, line_other), (1 - y, c, far_own), (1 - y, 1 - c, far_other),
+            ):
+                lane = pl.multiple_of(((source_z * 2 + at_y) * 2 + at_c) * piece, piece)
+                copy = pltpu.make_async_copy(
+                    ref.at[k], q.at[:, :, pl.ds(lane, piece), :], sems.at[len(copies)]
+                )
+                copy.start()
+                copies.append(copy)
+        for copy in copies:
+            copy.wait()
+
+    def turn_scores(h):
+        hs = slice(h * HD, (h + 1) * HD)
+        scores = lax.dot_general(turn_keys[0, :, hs], q[r, h], NT, preferred_element_type=F32)
+        key = own * page + lax.broadcasted_iota(jnp.int32, (page, lanes), 0)
+        token = lax.broadcasted_iota(jnp.int32, (page, lanes), 1) // group
+        return scores, key <= token
+
+    def begin(h, top):
+        hs = slice(h * HD, (h + 1) * HD)
+        scores, seen = turn_scores(h)
+        top = jnp.maximum(top, jnp.max(jnp.where(seen, scores, -1e30), axis=0, keepdims=True))
+        ref_exp = jnp.maximum(jnp.ceil(top * LOG2_SCALE), FLOOR_EXP)
+        weights = jnp.where(seen, jnp.exp2(scores * LOG2_SCALE - ref_exp), 0.0)
+        exps[h, 0:1, :] = ref_exp
+        sums[h, 0:1, :] = jnp.sum(weights, axis=0, keepdims=True)
+        acc[h] = lax.dot_general(
+            turn_values[0, :, hs], weights.astype(BF16), TN, preferred_element_type=F32
+        )
+
+    @pl.when(j == 0)
+    def _():
+        for h in range(kv_heads):
+            hs = slice(h * HD, (h + 1) * HD)
+            some = lax.dot_general(key_block[0, 0:128, hs], q[r, h], NT, preferred_element_type=F32)
+            live = lax.broadcasted_iota(jnp.int32, (128, lanes), 0) < n_first
+            begin(h, jnp.max(jnp.where(live, some, -1e30), axis=0, keepdims=True))
+
+    per = half // block
+    live_count = jnp.clip(jnp.where(j < per, n_first - j * block, n_second - (j - per) * block), 0, block)
+
+    def visit(masked):
+        for h in range(kv_heads):
+            hs = slice(h * HD, (h + 1) * HD)
+            scores = lax.dot_general(key_block[0, :, hs], q[r, h], NT, preferred_element_type=F32)
+            weights = jnp.exp2(scores * LOG2_SCALE - exps[h, 0:1, :])
+            if masked:
+                live = lax.broadcasted_iota(jnp.int32, (block, lanes), 0) < live_count
+                weights = jnp.where(live, weights, 0.0)
+            sums[h, 0:1, :] += jnp.sum(weights, axis=0, keepdims=True)
+            acc[h] += lax.dot_general(
+                value_block[0, :, hs], weights.astype(BF16), TN, preferred_element_type=F32
+            )
+
+    @pl.when(live_count == block)
+    def _():
+        visit(False)
+
+    @pl.when((live_count > 0) & (live_count < block))
+    def _():
+        visit(True)
+
+    @pl.when(j == pl.num_programs(1) - 1)
+    def _():
+        fine = functools.reduce(jnp.logical_and, [sums[h, 0:1, :] < SUM_LIMIT for h in range(kv_heads)])
+
+        @pl.when(jnp.max(jnp.where(fine, 0.0, 1.0)) > 0.5)
+        def _():
+            for h in range(kv_heads):
+                begin(h, jnp.full((1, lanes), -1e30, F32))
+            step = key_slab.shape[0]
+
+            def body(i, carry):
+                at = pl.multiple_of(i * step, step)
+                copy_k = pltpu.make_async_copy(all_keys.at[r, pl.ds(at, step), :], key_slab, sems.at[0])
+                copy_v = pltpu.make_async_copy(all_values.at[r, pl.ds(at, step), :], value_slab, sems.at[1])
+                copy_k.start()
+                copy_v.start()
+                copy_k.wait()
+                copy_v.wait()
+                slot = at + lax.broadcasted_iota(jnp.int32, (step, lanes), 0)
+                live = (slot < n_first) | ((slot >= half) & (slot < half + n_second))
+                for h in range(kv_heads):
+                    hs = slice(h * HD, (h + 1) * HD)
+                    scores = lax.dot_general(key_slab[:, hs], q[r, h], NT, preferred_element_type=F32)
+                    before = exps[h, 0:1, :]
+                    top = jnp.max(jnp.where(live, scores, -1e30), axis=0, keepdims=True)
+                    ref_exp = jnp.maximum(before, jnp.ceil(top * LOG2_SCALE))
+                    weights = jnp.where(live, jnp.exp2(scores * LOG2_SCALE - ref_exp), 0.0)
+                    shrink = jnp.exp2(before - ref_exp)
+                    exps[h, 0:1, :] = ref_exp
+                    sums[h, 0:1, :] = sums[h, 0:1, :] * shrink + jnp.sum(weights, axis=0, keepdims=True)
+                    acc[h] = acc[h] * shrink + lax.dot_general(
+                        value_slab[:, hs], weights.astype(BF16), TN, preferred_element_type=F32
+                    )
+                return carry
+
+            lax.fori_loop(0, history // step, body, 0)
+
+        for h in range(kv_heads):
+            out[0, h, 0:HD, :] = acc[h].astype(BF16)
+            out[0, h, HD:, :] = pack_stats(exps[h, 0:1, :], sums[h, 0:1, :])
+
+
+def attend(info, pieces, turn_keys, turn_values, cache_keys, cache_values, group):
+    grid_z, requests, kv_heads, piece, _ = pieces[0].shape
+    lanes = 4 * grid_z * piece
+    history, width = cache_keys.shape[1:]
+    half = history // 2
+    block = min(2048, half)
+    per = half // block
+    slab = min(256, half)
+
+    def request(step_r, info):
+        return lax.rem(step_r + info[7] + 1, 2)
+
+    def place(step_r, j, info):
+        r = request(step_r, info)
+        n_first, n_second = info[2 * r], info[2 * r + 1]
+        last_first = jnp.maximum((n_first + block - 1) // block, 1) - 1
+        last_second = per + (n_second + block - 1) // block - 1
+        second = jnp.where(n_second > 0, jnp.minimum(j, last_second), last_first)
+        return (r, jnp.where(j < per, jnp.minimum(j, last_first), second), 0)
+
+    def turn_place(step_r, j, info):
+        return (request(step_r, info), 0, 0)
+
+    anywhere = pl.BlockSpec(memory_space=pl.ANY)
+    turn_spec = pl.BlockSpec((1,) + turn_keys.shape[1:], turn_place)
+    cache_spec = pl.BlockSpec((1, block, width), place)
+    return pl.pallas_call(
+        functools.partial(attend_kernel, grid_z, group),
+        grid_spec=pltpu.PrefetchScalarGridSpec(
+            num_scalar_prefetch=1,
+            grid=(requests, 2 * per),
+            in_specs=[anywhere] * 4 + [turn_spec] * 2 + [cache_spec] * 2 + [anywhere] * 2,
+            out_specs=pl.BlockSpec((1, kv_heads, HD + STAT_ROWS, lanes), lambda s, j, info: (s, 0, 0, 0)),
+            scratch_shapes=[
+                pltpu.VMEM((requests, kv_heads, lanes, HD), BF16),
+                pltpu.VMEM((kv_heads, HD, lanes), F32),
+                pltpu.VMEM((kv_heads, 8, lanes), F32),
+                pltpu.VMEM((kv_heads, 8, lanes), F32),
+                pltpu.VMEM((slab, width), BF16),
+                pltpu.VMEM((slab, width), BF16),
+                pltpu.SemaphoreType.DMA((4 * grid_z,)),
+            ],
+        ),
+        out_shape=jax.ShapeDtypeStruct((requests, kv_heads, HD + STAT_ROWS, lanes), BF16),
+        compiler_params=pltpu.CompilerParams(vmem_limit_bytes=VMEM_LIMIT),
+        cost_estimate=pl.CostEstimate(
+            flops=4 * requests * kv_heads * lanes * history * HD,
+            bytes_accessed=4 * requests * history * width,
+            transcendentals=requests * kv_heads * lanes * history,
+        ),
+        name="attend",
+    )(info, *pieces, turn_keys, turn_values, cache_keys, cache_values, cache_keys, cache_values)
+
+
+def merge_cores_kernel(info, mine, got, keep, send):
+    z, y = info[5], info[6]
+    kv_heads, _, lanes = got.shape
+    half = lanes // 2
+    for out, which in ((keep, y), (send, 1 - y)):
+        at = pl.ds(pl.multiple_of(which * half, half), half)
+        for k in range(kv_heads):
+            h = lax.rem(z + k, kv_heads)
+            summed, top, total = combine([mine[1, h, :, at], got[h, :, at]])
+            out[k, 0:HD, :] = summed.astype(BF16)
+            out[k, HD:, :] = pack_stats(top, total)
+
+
+def merge_rows_kernel(mine, got, *outs):
+    for k, out in enumerate(outs):
+        summed, top, total = combine([mine[k], got[k]])
+        out[0:HD, :] = summed.astype(BF16)
+        out[HD:, :] = pack_stats(top, total)
+
+
+def finish_kernel(group, *refs):
+    parts, (out, turned) = refs[:-2], refs[-2:]
+    summed, _, total = combine([part[...] for part in parts])
+    turned[...] = jnp.transpose(summed / total)
+    tokens = out.shape[0]
+    for g in range(group):
+        out[:, g * HD : (g + 1) * HD] = turned[pl.ds(g, tokens, stride=group), :].astype(BF16)
+
+
+def project_kernel(grid_z, count, info, *refs):
+    rows_refs, (weight, out, joined) = refs[:count], refs[count:]
+    z, y, c = info[5], info[6], info[7]
+    step = pl.program_id(0)
+
+    tokens, width = rows_refs[0].shape
+
+    @pl.when(step == 0)
+    def _():
+        out[...] = jnp.zeros_like(out)
+        for i, ref in enumerate(rows_refs):
+            k, dy, dc = i // 4, (i // 2) % 2, i % 2
+            source_z = lax.rem(z - k + grid_z, grid_z)
+            at_y = jnp.where(dy == 1, 1 - y, y)
+            at_c = jnp.where(dc == 1, 1 - c, c)
+            row = pl.multiple_of((at_y * 2 + at_c) * tokens, tokens)
+            joined[source_z, pl.ds(row, tokens), :] = ref[...]
+
+    out[...] += jnp.dot(joined[step], weight[...], preferred_element_type=F32)
+
+
+def fast_on_device(
+    grid_z, queries, new_keys, new_values, cache_keys, cache_values, hist_len, page_owner, out_weight
+):
+    members = lax.axis_size("ctx")
+    own = lax.axis_index("ctx")
+    z, y, c = own // 4, (own // 2) % 2, own % 2
+    requests, page_rows, kv_width = new_keys.shape
+    kv_heads = kv_width // HD
+    group = queries.shape[2] // kv_width
+    half = cache_keys.shape[1] // 2
+    lanes = members * page_rows * group
+
+    def hop_z(array, k):
+        return lax.ppermute(array, "ctx", [(i, (i + 4 * k) % members) for i in range(members)])
+
+    def hop_y(array):
+        return lax.ppermute(array, "ctx", [(i, i ^ 2) for i in range(members)])
+
+    def hop_core(array):
+        return lax.ppermute(array, "ctx", [(i, i ^ 1) for i in range(members)])
+
+    owner_row = lax.dynamic_index_in_dim(page_owner, own, 1, keepdims=False)
+    targets = (owner_row[None, :] == jnp.arange(members, dtype=jnp.int32)[:, None]).astype(BF16)
+    both = jnp.concatenate([new_keys, new_values], axis=2)
+    pages = lax.psum_scatter(
+        targets[:, :, None, None] * both[None], "ctx", scatter_dimension=0, tiled=True
+    )
+
+    first = own * half
+    second = (2 * members - 1 - own) * half
+    counts = jnp.stack(
+        [jnp.clip(hist_len - first, 0, half), jnp.clip(hist_len - second, 0, half)], axis=1
+    ).reshape(-1)
+    info = jnp.concatenate([counts, jnp.stack([own, z, y, c])]).astype(jnp.int32)
+
+    piece = queries.reshape(page_rows, requests, kv_heads, group, HD)
+    piece = piece.transpose(1, 2, 0, 3, 4).reshape(requests, kv_heads, page_rows * group, HD)
+    line_own = jnp.stack([piece] + [hop_z(piece, k) for k in range(1, grid_z)])
+    far_own = hop_y(line_own)
+    line_other = hop_core(line_own)
+    far_other = hop_core(far_own)
+    partial = attend(
+        info, (line_own, line_other, far_own, far_other), new_keys, new_values, cache_keys, cache_values, group
+    )
+    rows = HD + STAT_ROWS
+    smem = pl.BlockSpec(memory_space=pltpu.SMEM)
+    vmem = pl.BlockSpec(memory_space=pltpu.VMEM)
+    params = pltpu.CompilerParams(vmem_limit_bytes=VMEM_LIMIT)
+    half_shape = jax.ShapeDtypeStruct((kv_heads, rows, lanes // 2), BF16)
+    keep, send = pl.pallas_call(
+        merge_cores_kernel, in_specs=[smem, vmem, vmem], out_specs=[vmem, vmem],
+        out_shape=[half_shape, half_shape], compiler_params=params, name="merge_cores",
+    )(info, partial, hop_core(partial[0]))
+    parts = pl.pallas_call(
+        merge_rows_kernel, in_specs=[vmem, vmem], out_specs=[vmem] * grid_z,
+        out_shape=[jax.ShapeDtypeStruct((rows, lanes // 2), BF16)] * grid_z,
+        compiler_params=params, name="merge_rows",
+    )(keep, hop_y(send))
+    tokens = members * page_rows // 2
+    own_rows = pl.pallas_call(
+        functools.partial(finish_kernel, group), in_specs=[vmem] * grid_z, out_specs=vmem,
+        out_shape=jax.ShapeDtypeStruct((tokens, group * HD), BF16),
+        scratch_shapes=[pltpu.VMEM((tokens * group, HD), F32)],
+        compiler_params=params, name="finish",
+    )(parts[0], *[hop_z(parts[k], k) for k in range(1, grid_z)])
+
+    all_rows = []
+    for k in range(grid_z):
+        near = own_rows if k == 0 else hop_z(own_rows, k)
+        far = hop_y(near)
+        all_rows += [near, hop_core(near), far, hop_core(far)]
+    columns = out_weight.shape[1]
+    full = pl.BlockSpec((tokens, group * HD), lambda s: (0, 0))
+    projected = pl.pallas_call(
+        functools.partial(project_kernel, grid_z, len(all_rows)),
+        grid=(grid_z,),
+        in_specs=[smem] + [full] * len(all_rows) + [pl.BlockSpec((group * HD, columns), lambda s: (s, 0))],
+        out_specs=pl.BlockSpec((4 * tokens, columns), lambda s: (0, 0)),
+        out_shape=jax.ShapeDtypeStruct((4 * tokens, columns), F32),
+        scratch_shapes=[pltpu.VMEM((grid_z, 4 * tokens, group * HD), BF16)],
+        compiler_params=params, name="project",
+    )(info, *all_rows, out_weight)
+    halves = projected.reshape(2, requests, tokens, columns)
+    side = lax.axis_index("tp")
+    stay = lax.dynamic_index_in_dim(halves, side, 0, keepdims=False)
+    leave = lax.dynamic_index_in_dim(halves, 1 - side, 0, keepdims=False)
+    arrived = lax.ppermute(leave.astype(BF16), "tp", [(0, 1), (1, 0)])
+    attended = (stay + arrived.astype(F32)).astype(BF16).transpose(1, 0, 2)
+    return attended, pages[:, :, :, :kv_width], pages[:, :, :, kv_width:]
+
+
 def solution(mesh):
-    return jax.shard_map(
-        on_device,
-        mesh=mesh,
-        in_specs=(
-            P("ctx", None, "tp"),
-            P(None, "ctx", "tp"),
-            P(None, "ctx", "tp"),
-            P(None, "ctx", "tp"),
-            P(None, "ctx", "tp"),
-            P(),
-            P(),
-            P("tp", "ctx"),
-        ),
-        out_specs=(P("tp", None, "ctx"), P("ctx", None, None, "tp"), P("ctx", None, None, "tp")),
-        check_vma=False,
-    )
+    members, sides = mesh.shape["ctx"], mesh.shape["tp"]
+
+    def run(queries, new_keys, *others):
+        requests, _, width = new_keys.shape
+        kv_heads = width // HD // sides
+        staged = members % 4 == 0 and requests == 2 and sides == 2 and kv_heads == members // 4
+        body = functools.partial(fast_on_device, members // 4) if staged else on_device
+        return jax.shard_map(
+            body,
+            mesh=mesh,
+            in_specs=(
+                P("ctx", None, "tp"),
+                P(None, "ctx", "tp"),
+                P(None, "ctx", "tp"),
+                P(None, "ctx", "tp"),
+                P(None, "ctx", "tp"),
+                P(),
+                P(),
+                P("tp", "ctx"),
+            ),
+            out_specs=(P("tp", None, "ctx"), P("ctx", None, None, "tp"), P("ctx", None, None, "tp")),
+            check_vma=False,
+        )(queries, new_keys, *others)
+
+    return run

time: 396 us -> 283 us (0.71)
  blocking collectives: 117 us -> 0 us
  Pallas kernels: 0 us -> 72.6 us
  starting transfers between devices: 11.1 us -> 71.9 us
  matrix products: 43.1 us -> 0 us
  local copies, waits for them, and re-layouts: 47.5 us -> 12.3 us
  waiting for transfers between devices: 136 us -> 109 us
  other arithmetic: 25.3 us -> 2.4 us
    unnamed x4 -> x2, waiting for transfers between devices: 0.73 us -> 79.2 us
    pallas_call x0 -> x5, Pallas kernels: none -> 72.6 us  [the longest x1 61.9 us: attend(): pl.pallas_call(functools.partial(attend_kernel, grid_z, group), grid_spec...]
    ppermute x0 -> x27, starting transfers between devices: none -> 71.9 us  [the longest x9 57.1 us: hop_z(): lax.ppermute(array, 'ctx', [(i, (i + 4 * k) % members) for i in range(mem...]
    reduce_scatter x2 -> x0, waiting for transfers between devices: 69.7 us -> none  [the longest x1 58.9 us: on_device(): lax.psum_scatter(accumulated * (weight / global_total)[..., None], 'ctx',...]
    pmax x1 -> x0, blocking collectives: 59.6 us -> none  [on_device(): global_peak = lax.pmax(peak_score, 'ctx')]
    psum x1 -> x0, blocking collectives: 57.6 us -> none  [on_device(): global_total = lax.psum(running_total * weight, 'ctx')]
    all_gather x2 -> x0, waiting for transfers between devices: 52 us -> none  [the longest x1 38.3 us: on_device(): lax.all_gather(shared_rows.astype(jnp.bfloat16), 'ctx', axis=0, tiled=True)]
    dot_general x19 -> x0, matrix products: 43.1 us -> none  [the longest x9 26.2 us: online_step(): jnp.einsum('nrkgb,rbkd->nrkgd', weights.astype(jnp.bfloat16), value_block...]
  transfers between devices with their start and end apart: 6 -> 28, of which waited for: 6 -> 15; matrix products, arithmetic and copies ran while one was open for 1% -> 2% of each run, Pallas kernels for 0% -> 0%
where the time goes in v1:
time: 283 us
  waiting for transfers between devices  109 us (39%)
  Pallas kernels  72.6 us (26%)
  starting transfers between devices  71.9 us (25%)
  between operations  14.3 us (5%)
  local copies, waits for them, and re-layouts  12.3 us (4%)
    unnamed x2, waiting for transfers between devices  79.2 us
    pallas_call x1, Pallas kernels, attend(): pl.pallas_call(functools.partial(attend_kernel, grid_z, group), grid_spec...  61.9 us
    ppermute x9, starting transfers between devices, hop_z(): lax.ppermute(array, 'ctx', [(i, (i + 4 * k) % members) for i in range(mem...  57.1 us
    ppermute x6, waiting for transfers between devices, hop_y(): return lax.ppermute(array, 'ctx', [(i, i ^ 2) for i in range(members)])  15.4 us
    ppermute x6, starting transfers between devices, hop_y(): return lax.ppermute(array, 'ctx', [(i, i ^ 2) for i in range(members)])  12.1 us
    ppermute x9, waiting for transfers between devices, hop_z(): lax.ppermute(array, 'ctx', [(i, (i + 4 * k) % members) for i in range(mem...  10.4 us
  transfers between devices with their start and end apart: 28, of which 15 were waited for; matrix products, arithmetic and copies ran while one was open for 2% of the time, Pallas kernels for 0%

profile of v1, /device:TPU:0, one launch (start us, length us, event | category | flops | bytes accessed | tf_op | source)
XLA Modules:
  0.0 282.7 jit_solution(228785308025903359)
XLA Ops:
  8.1 4.1 %collective-permute-start.1 = (bf16[2,4,32,128]{3,2,1,0:T(8,128)(2,1)S(1)}, bf16[2,4,32,128]{3,2,1,0:T(8,128)(2,1)S(1)}, u32[]{:S(2)}, u32[]{:S(2)}) collective-permute-start(bf16[2,4,32,128]{3,2,1,0:T(8,128)(2,1)S(1)} %bitcast.36), channel_id=1, source_target_pairs={{0,16},{2,18},{4,20},{6,22},{8,24},{10,26},{12,28},{14,30},{16,0},... | collective-permute-start | bytes 196616 | tf_op jit(solution)/shard_map/ppermute | solution.py:398
  12.2 1.3 collective-permute-start.2
  16.5 3.1 %collective-permute-done = bf16[2,4,32,128]{3,2,1,0:T(8,128)(2,1)S(1)} collective-permute-done((bf16[2,4,32,128]{3,2,1,0:T(8,128)(2,1)S(1)}, bf16[2,4,32,128]{3,2,1,0:T(8,128)(2,1)S(1)}, u32[]{:S(2)}, u32[]{:S(2)}) %collective-permute-start) | collective-permute-done | bytes 65568 | tf_op jit(solution)/shard_map/ppermute | solution.py:398
  19.7 1.6 collective-permute-start.4
  21.3 4.9 %collective-permute-done.4.far_own = bf16[4,2,4,32,128]{4,3,2,1,0:T(8,128)(2,1)S(1)} collective-permute-done((bf16[4,2,4,32,128]{4,3,2,1,0:T(8,128)(2,1)S(1)}, bf16[4,2,4,32,128]{4,3,2,1,0:T(8,128)(2,1)S(1)}, u32[]{:S(2)}, u32[]{:S(2)}) %collective-permute-start.4) | collective-permute-done | bytes 262176 | tf_op jit(solution)/shard_map/ppermute | solution.py:401
  29.2 61.9 %attend.1.mine = bf16[2,4,144,512]{3,2,1,0:T(8,128)(2,1)} custom-call(s32[8]{0:T(128)} %concatenate.6.info, bf16[4,2,4,32,128]{4,3,2,1,0:T(8,128)(2,1)} %copy-done.1, bf16[4,2,4,32,128]{4,3,2,1,0:T(8,128)(2,1)} %copy-done.5, bf16[4,2,4,32,128]{4,3,2,1,0:T(8,128)(2,1)} %copy-done.4, bf16[4,2,4,32,128]{4,3,2,1,0:T(8,128)(2,1)} %copy-done.6, ...), custom_call_target="tpu_custom_call" | custom-call | flops 8589934592 | bytes 16777216 | tf_op jit(solution)/shard_map/attend/pallas_call | solution.py:307
  92.3 2.0 collective-permute-done.6.got
  95.1 2.5 merge_cores.1
  97.6 6.0 %collective-permute-start.7 = (bf16[4,144,256]{2,1,0:T(8,128)(2,1)}, bf16[4,144,256]{2,1,0:T(8,128)(2,1)S(1)}, u32[]{:S(2)}, u32[]{:S(2)}) collective-permute-start(bf16[4,144,256]{2,1,0:T(8,128)(2,1)} %get-tuple-element.10), channel_id=1, source_target_pairs={{0,4},{2,6},{4,0},{6,2},{8,12},{10,14},{12,8},{14,10},{16,20},{18,... | collective-permute-start | bytes 884744 | tf_op jit(solution)/shard_map/ppermute | solution.py:401
  103.8 7.3 %collective-permute-done.7.got = bf16[4,144,256]{2,1,0:T(8,128)(2,1)S(1)} collective-permute-done((bf16[4,144,256]{2,1,0:T(8,128)(2,1)}, bf16[4,144,256]{2,1,0:T(8,128)(2,1)S(1)}, u32[]{:S(2)}, u32[]{:S(2)}) %collective-permute-start.7) | collective-permute-done | bytes 294944 | tf_op jit(solution)/shard_map/ppermute | solution.py:401
  111.8 1.8 merge_rows.1
  113.6 45.2 %collective-permute-start.8 = (bf16[144,256]{1,0:T(8,128)(2,1)}, bf16[144,256]{1,0:T(8,128)(2,1)S(1)}, u32[]{:S(2)}, u32[]{:S(2)}) collective-permute-start(bf16[144,256]{1,0:T(8,128)(2,1)} %get-tuple-element.12), channel_id=1, source_target_pairs={{0,8},{2,10},{4,12},{6,14},{8,16},{10,18},{12,20},{14,22},{16,24},... | collective-permute-start | bytes 221192 | tf_op jit(solution)/shard_map/ppermute | solution.py:398
  158.9 1.5 collective-permute-start.9
  161.7 3.4 %collective-permute-done.9.refs_2_ = bf16[144,256]{1,0:T(8,128)(2,1)S(1)} collective-permute-done((bf16[144,256]{1,0:T(8,128)(2,1)}, bf16[144,256]{1,0:T(8,128)(2,1)S(1)}, u32[]{:S(2)}, u32[]{:S(2)}) %collective-permute-start.9) | collective-permute-done | bytes 73760 | tf_op jit(solution)/shard_map/ppermute | solution.py:398
  165.7 1.8 finish.1.refs_0_
  167.5 1.3 collective-permute-start.14
  168.8 2.2 collective-permute-start.18
  171.8 1.4 collective-permute-start.12
  179.1 1.5 collective-permute-done.20.refs_10_
  182.4 79.2 %all-reduce.3.cloned.1.call-done = bf16[16,2,4,1024]{3,2,1,0:T(4,128)(2,1)} async-done(((bf16[16,2,4,1024]{3,2,1,0:T(4,128)(2,1)}), bf16[16,2,4,1024]{3,2,1,0:T(4,128)(2,1)}) %all-reduce.3.cloned.1.call-update) | async-done | bytes 262160
  261.6 2.0 constant_dynamic-slice_fusion.2
  264.9 4.6 %project.1 = f32[128,512]{1,0:T(8,128)} custom-call(s32[8]{0:T(128)} %concatenate.6.info, bf16[32,1024]{1,0:T(8,128)(2,1)} %finish.1.refs_0_, bf16[32,1024]{1,0:T(8,128)(2,1)} %copy-done.14, bf16[32,1024]{1,0:T(8,128)(2,1)} %copy-done.13, bf16[32,1024]{1,0:T(8,128)(2,1)} %copy-done.18, bf16[32,1024]{1,0:T(8,128)(2,1)} %copy-done.10, ...), custom_call_target="tpu_custom_call" | custom-call | tf_op jit(solution)/shard_map/project/pallas_call | solution.py:458
  270.5 1.5 collective-permute-start.26
  273.0 2.1 collective-permute-done.26
  (113 shorter events, 23.9 us)
Async XLA Ops:
  7.2 254.4 %all-reduce.3.cloned.1.call-start = ((), (), s32[]{:S(2)}) async-start(), calls=%async_computation | async-start | bytes 524288
  8.1 7.2 %collective-permute-start.1 = (bf16[2,4,32,128]{3,2,1,0:T(8,128)(2,1)S(1)}, bf16[2,4,32,128]{3,2,1,0:T(8,128)(2,1)S(1)}, u32[]{:S(2)}, u32[]{:S(2)}) collective-permute-start(bf16[2,4,32,128]{3,2,1,0:T(8,128)(2,1)S(1)} %bitcast.36), channel_id=1, source_target_pairs={{0,16},{2,18},{4,20},{6,22},{8,24},{10,26},{12,28},{14,30},{16,0},... | collective-permute-start | bytes 196616 | tf_op jit(solution)/shard_map/ppermute | solution.py:398
  13.6 6.1 %collective-permute-start = (bf16[2,4,32,128]{3,2,1,0:T(8,128)(2,1)S(1)}, bf16[2,4,32,128]{3,2,1,0:T(8,128)(2,1)S(1)}, u32[]{:S(2)}, u32[]{:S(2)}) collective-permute-start(bf16[2,4,32,128]{3,2,1,0:T(8,128)(2,1)S(1)} %bitcast.38), channel_id=1, source_target_pairs={{0,8},{2,10},{4,12},{6,14},{8,16},{10,18},{12,20},{14,22},{16,24},... | collective-permute-start | bytes 196616 | tf_op jit(solution)/shard_map/ppermute | solution.py:398
  19.7 6.5 %collective-permute-start.4 = (bf16[4,2,4,32,128]{4,3,2,1,0:T(8,128)(2,1)S(1)}, bf16[4,2,4,32,128]{4,3,2,1,0:T(8,128)(2,1)S(1)}, u32[]{:S(2)}, u32[]{:S(2)}) collective-permute-start(bf16[4,2,4,32,128]{4,3,2,1,0:T(8,128)(2,1)S(1)} %pad_maximum_fusion.line_own), channel_id=1, source_target_pairs={{0,4},{2,6},{4,0},{6,2},{8,12},{10,14},{12,8},{14,10},{16,20},{18,... | collective-permute-start | bytes 786440 | tf_op jit(solution)/shard_map/ppermute | solution.py:401
  21.3 6.4 %collective-permute-start.3 = (bf16[4,2,4,32,128]{4,3,2,1,0:T(8,128)(2,1)S(1)}, bf16[4,2,4,32,128]{4,3,2,1,0:T(8,128)(2,1)S(1)}, u32[]{:S(2)}, u32[]{:S(2)}) collective-permute-start(bf16[4,2,4,32,128]{4,3,2,1,0:T(8,128)(2,1)S(1)} %pad_maximum_fusion.line_own), channel_id=1, source_target_pairs={{0,2},{2,0},{4,6},{6,4},{8,10},{10,8},{12,14},{14,12},{16,18},{18,... | collective-permute-start | bytes 786440 | tf_op jit(solution)/shard_map/ppermute | solution.py:404
  97.6 13.5 %collective-permute-start.7 = (bf16[4,144,256]{2,1,0:T(8,128)(2,1)}, bf16[4,144,256]{2,1,0:T(8,128)(2,1)S(1)}, u32[]{:S(2)}, u32[]{:S(2)}) collective-permute-start(bf16[4,144,256]{2,1,0:T(8,128)(2,1)} %get-tuple-element.10), channel_id=1, source_target_pairs={{0,4},{2,6},{4,0},{6,2},{8,12},{10,14},{12,8},{14,10},{16,20},{18,... | collective-permute-start | bytes 884744 | tf_op jit(solution)/shard_map/ppermute | solution.py:401
  113.6 47.8 %collective-permute-start.10 = (bf16[144,256]{1,0:T(8,128)(2,1)}, bf16[144,256]{1,0:T(8,128)(2,1)S(1)}, u32[]{:S(2)}, u32[]{:S(2)}) collective-permute-start(bf16[144,256]{1,0:T(8,128)(2,1)} %get-tuple-element.14), channel_id=1, source_target_pairs={{0,24},{2,26},{4,28},{6,30},{8,0},{10,2},{12,4},{14,6},{16,8},{18,... | collective-permute-start | bytes 221192 | tf_op jit(solution)/shard_map/ppermute | solution.py:398
  113.6 48.0 %collective-permute-start.8 = (bf16[144,256]{1,0:T(8,128)(2,1)}, bf16[144,256]{1,0:T(8,128)(2,1)S(1)}, u32[]{:S(2)}, u32[]{:S(2)}) collective-permute-start(bf16[144,256]{1,0:T(8,128)(2,1)} %get-tuple-element.12), channel_id=1, source_target_pairs={{0,8},{2,10},{4,12},{6,14},{8,16},{10,18},{12,20},{14,22},{16,24},... | collective-permute-start | bytes 221192 | tf_op jit(solution)/shard_map/ppermute | solution.py:398
  158.9 6.2 %collective-permute-start.9 = (bf16[144,256]{1,0:T(8,128)(2,1)}, bf16[144,256]{1,0:T(8,128)(2,1)S(1)}, u32[]{:S(2)}, u32[]{:S(2)}) collective-permute-start(bf16[144,256]{1,0:T(8,128)(2,1)} %get-tuple-element.13), channel_id=1, source_target_pairs={{0,16},{2,18},{4,20},{6,22},{8,24},{10,26},{12,28},{14,30},{16,0},... | collective-permute-start | bytes 221192 | tf_op jit(solution)/shard_map/ppermute | solution.py:398
  167.5 6.6 %collective-permute-start.14 = (bf16[32,1024]{1,0:T(8,128)(2,1)}, bf16[32,1024]{1,0:T(8,128)(2,1)S(1)}, u32[]{:S(2)}, u32[]{:S(2)}) collective-permute-start(bf16[32,1024]{1,0:T(8,128)(2,1)} %finish.1.refs_0_), channel_id=1, source_target_pairs={{0,8},{2,10},{4,12},{6,14},{8,16},{10,18},{12,20},{14,22},{16,24},... | collective-permute-start | bytes 196616 | tf_op jit(solution)/shard_map/ppermute | solution.py:398
  168.8 6.6 %collective-permute-start.18 = (bf16[32,1024]{1,0:T(8,128)(2,1)}, bf16[32,1024]{1,0:T(8,128)(2,1)S(1)}, u32[]{:S(2)}, u32[]{:S(2)}) collective-permute-start(bf16[32,1024]{1,0:T(8,128)(2,1)} %finish.1.refs_0_), channel_id=1, source_target_pairs={{0,16},{2,18},{4,20},{6,22},{8,24},{10,26},{12,28},{14,30},{16,0},... | collective-permute-start | bytes 196616 | tf_op jit(solution)/shard_map/ppermute | solution.py:398
  171.1 5.5 %collective-permute-start.22 = (bf16[32,1024]{1,0:T(8,128)(2,1)}, bf16[32,1024]{1,0:T(8,128)(2,1)S(1)}, u32[]{:S(2)}, u32[]{:S(2)}) collective-permute-start(bf16[32,1024]{1,0:T(8,128)(2,1)} %finish.1.refs_0_), channel_id=1, source_target_pairs={{0,24},{2,26},{4,28},{6,30},{8,0},{10,2},{12,4},{14,6},{16,8},{18,... | collective-permute-start | bytes 196616 | tf_op jit(solution)/shard_map/ppermute | solution.py:398
  171.8 5.7 %collective-permute-start.12 = (bf16[32,1024]{1,0:T(8,128)(2,1)}, bf16[32,1024]{1,0:T(8,128)(2,1)S(1)}, u32[]{:S(2)}, u32[]{:S(2)}) collective-permute-start(bf16[32,1024]{1,0:T(8,128)(2,1)} %finish.1.refs_0_), channel_id=1, source_target_pairs={{0,4},{2,6},{4,0},{6,2},{8,12},{10,14},{12,8},{14,10},{16,20},{18,... | collective-permute-start | bytes 196616 | tf_op jit(solution)/shard_map/ppermute | solution.py:401
  174.2 5.0 %collective-permute-start.16 = (bf16[32,1024]{1,0:T(8,128)(2,1)S(1)}, bf16[32,1024]{1,0:T(8,128)(2,1)S(1)}, u32[]{:S(2)}, u32[]{:S(2)}) collective-permute-start(bf16[32,1024]{1,0:T(8,128)(2,1)S(1)} %collective-permute-done.14.refs_4_), channel_id=1, source_target_pairs={{0,4},{2,6},{4,0},{6,2},{8,12},{10,14},{12,8},{14,10},{16,20},{18,... | collective-permute-start | bytes 196616 | tf_op jit(solution)/shard_map/ppermute | solution.py:401
  175.4 5.2 %collective-permute-start.20 = (bf16[32,1024]{1,0:T(8,128)(2,1)S(1)}, bf16[32,1024]{1,0:T(8,128)(2,1)S(1)}, u32[]{:S(2)}, u32[]{:S(2)}) collective-permute-start(bf16[32,1024]{1,0:T(8,128)(2,1)S(1)} %collective-permute-done.18.refs_8_), channel_id=1, source_target_pairs={{0,4},{2,6},{4,0},{6,2},{8,12},{10,14},{12,8},{14,10},{16,20},{18,... | collective-permute-start | bytes 196616 | tf_op jit(solution)/shard_map/ppermute | solution.py:401
  176.6 5.2 %collective-permute-start.24 = (bf16[32,1024]{1,0:T(8,128)(2,1)S(1)}, bf16[32,1024]{1,0:T(8,128)(2,1)S(1)}, u32[]{:S(2)}, u32[]{:S(2)}) collective-permute-start(bf16[32,1024]{1,0:T(8,128)(2,1)S(1)} %collective-permute-done.22.refs_12_), channel_id=1, source_target_pairs={{0,4},{2,6},{4,0},{6,2},{8,12},{10,14},{12,8},{14,10},{16,20},{18,... | collective-permute-start | bytes 196616 | tf_op jit(solution)/shard_map/ppermute | solution.py:401
  177.5 4.3 %collective-permute-start.13 = (bf16[32,1024]{1,0:T(8,128)(2,1)S(1)}, bf16[32,1024]{1,0:T(8,128)(2,1)S(1)}, u32[]{:S(2)}, u32[]{:S(2)}) collective-permute-start(bf16[32,1024]{1,0:T(8,128)(2,1)S(1)} %collective-permute-done.12.refs_2_), channel_id=1, source_target_pairs={{0,2},{2,0},{4,6},{6,4},{8,10},{10,8},{12,14},{14,12},{16,18},{18,... | collective-permute-start | bytes 196616 | tf_op jit(solution)/shard_map/ppermute | solution.py:404
  177.5 4.8 %collective-permute-start.15 = (bf16[32,1024]{1,0:T(8,128)(2,1)S(1)}, bf16[32,1024]{1,0:T(8,128)(2,1)S(1)}, u32[]{:S(2)}, u32[]{:S(2)}) collective-permute-start(bf16[32,1024]{1,0:T(8,128)(2,1)S(1)} %collective-permute-done.14.refs_4_), channel_id=1, source_target_pairs={{0,2},{2,0},{4,6},{6,4},{8,10},{10,8},{12,14},{14,12},{16,18},{18,... | collective-permute-start | bytes 196616 | tf_op jit(solution)/shard_map/ppermute | solution.py:404
  179.1 84.5 %collective-permute-start.19 = (bf16[32,1024]{1,0:T(8,128)(2,1)S(1)}, bf16[32,1024]{1,0:T(8,128)(2,1)S(1)}, u32[]{:S(2)}, u32[]{:S(2)}) collective-permute-start(bf16[32,1024]{1,0:T(8,128)(2,1)S(1)} %collective-permute-done.18.refs_8_), channel_id=1, source_target_pairs={{0,2},{2,0},{4,6},{6,4},{8,10},{10,8},{12,14},{14,12},{16,18},{18,... | collective-permute-start | bytes 196616 | tf_op jit(solution)/shard_map/ppermute | solution.py:404
  180.6 82.9 %collective-permute-start.23 = (bf16[32,1024]{1,0:T(8,128)(2,1)S(1)}, bf16[32,1024]{1,0:T(8,128)(2,1)S(1)}, u32[]{:S(2)}, u32[]{:S(2)}) collective-permute-start(bf16[32,1024]{1,0:T(8,128)(2,1)S(1)} %collective-permute-done.22.refs_12_), channel_id=1, source_target_pairs={{0,2},{2,0},{4,6},{6,4},{8,10},{10,8},{12,14},{14,12},{16,18},{18,... | collective-permute-start | bytes 196616 | tf_op jit(solution)/shard_map/ppermute | solution.py:404
  181.8 81.8 %collective-permute-start.17 = (bf16[32,1024]{1,0:T(8,128)(2,1)S(1)}, bf16[32,1024]{1,0:T(8,128)(2,1)S(1)}, u32[]{:S(2)}, u32[]{:S(2)}) collective-permute-start(bf16[32,1024]{1,0:T(8,128)(2,1)S(1)} %collective-permute-done.16.refs_6_), channel_id=1, source_target_pairs={{0,2},{2,0},{4,6},{6,4},{8,10},{10,8},{12,14},{14,12},{16,18},{18,... | collective-permute-start | bytes 196616 | tf_op jit(solution)/shard_map/ppermute | solution.py:404
  181.8 81.8 %collective-permute-start.21 = (bf16[32,1024]{1,0:T(8,128)(2,1)S(1)}, bf16[32,1024]{1,0:T(8,128)(2,1)S(1)}, u32[]{:S(2)}, u32[]{:S(2)}) collective-permute-start(bf16[32,1024]{1,0:T(8,128)(2,1)S(1)} %collective-permute-done.20.refs_10_), channel_id=1, source_target_pairs={{0,2},{2,0},{4,6},{6,4},{8,10},{10,8},{12,14},{14,12},{16,18},{18,... | collective-permute-start | bytes 196616 | tf_op jit(solution)/shard_map/ppermute | solution.py:404
  182.3 81.3 %collective-permute-start.25 = (bf16[32,1024]{1,0:T(8,128)(2,1)S(1)}, bf16[32,1024]{1,0:T(8,128)(2,1)S(1)}, u32[]{:S(2)}, u32[]{:S(2)}) collective-permute-start(bf16[32,1024]{1,0:T(8,128)(2,1)S(1)} %collective-permute-done.24.refs_14_), channel_id=1, source_target_pairs={{0,2},{2,0},{4,6},{6,4},{8,10},{10,8},{12,14},{14,12},{16,18},{18,... | collective-permute-start | bytes 196616 | tf_op jit(solution)/shard_map/ppermute | solution.py:404
  270.5 4.6 %collective-permute-start.26 = (bf16[2,32,512]{2,0,1:T(2,128)(2,1)S(1)}, bf16[2,32,512]{2,0,1:T(2,128)(2,1)S(1)}, u32[]{:S(2)}, u32[]{:S(2)}) collective-permute-start(bf16[2,32,512]{2,0,1:T(2,128)(2,1)S(1)} %bitcast.40), channel_id=1, source_target_pairs={{0,1},{1,0},{2,3},{3,2},{4,5},{5,4},{6,7},{7,6},{8,9},{9,8},{10,11... | collective-permute-start | bytes 196616 | tf_op jit(solution)/shard_map/ppermute | solution.py:471
  (32 other events, 1334.2 us)
Sparse Core Ops, SparseCore 0:
  174.3 87.2 all-reduce.2
